TPU v7x, 32 devices: a whole 2x2x4 slice. The times are simulated.
32 devices in a mesh: space: 8 (over y, x, core), view: 4 (over z).
Axes of the slice: x: 2, y: 2, z: 4, core: 2. Of those that a mesh axis runs over, the one named last changes fastest.
Arguments:
- estimate: float32 [512, 32, 256], P('space'), may hold values from 0.5 to 2
- images: bfloat16 [8, 512, 32, 256], P('view', 'space'), may hold values from 0.5 to 2
- kernel_halves: float32 [8, 3, 16], P('view'), may hold values from 0.02 to 1
Outputs:
- new_estimate: float32 [512, 32, 256], P('space', 'view')
All inputs are finite; a program needn't handle non-finite values.
Results may differ from a plain program's by a relative error of at most 0.0003.
Values sent between devices are 32-bit elements; how exact they have to be, the bound alone decides.
A program may use at most 128 MiB of HBM per device.

v0:
```python
import functools

import jax
import jax.numpy as jnp
from jax import lax
from jax.experimental import pallas as pl
from jax.experimental.pallas import tpu as pltpu
from jax.sharding import PartitionSpec as P

ITERS = 2
MARGIN = 16
UNIT = 16
STEP = 8
MESH = pl.DeviceIdType.MESH
F32, BF16 = jnp.float32, jnp.bfloat16
ORDERS = ((1, 2, 0, 3), (2, 1, 0, 3))


def halved(t):
    hi = t.astype(BF16)
    return hi, (t - hi.astype(F32)).astype(BF16)


def thirds(t):
    hi = t.astype(BF16)
    rest = t - hi.astype(F32)
    mid = rest.astype(BF16)
    return hi, mid, (rest - mid.astype(F32)).astype(BF16)


def dot(a, b):
    return jnp.dot(a, b, preferred_element_type=F32)


def aligned(start, multiple=STEP):
    return start if isinstance(start, int) else pl.multiple_of(start, multiple)


def kernel(dims, est_hbm, img_hbm, halves, out, cur, mid, smooth, fac, from_l, from_r, to_r, to_l, eland, est, img,
           ty, cx, dm, pm, local_sem, est_send, est_recv, halo_send, halo_recv, edge_send, edge_recv,
           send_r, recv_l, send_l, recv_r):
    n, planes, wx, wy, views, taps = dims
    me = lax.axis_index("view")
    spot, spots = lax.axis_index("space"), lax.axis_size("space")
    has_down, has_up = spot > 0, spot < spots - 1
    has_left, has_right = me > 0, me < n - 1
    up = {"space": jnp.minimum(spot + 1, spots - 1)}
    down = {"space": jnp.maximum(spot - 1, 0)}
    right = {"view": jnp.minimum(me + 1, n - 1)}
    left = {"view": jnp.maximum(me - 1, 0)}
    rows = wx // n
    tile = wx * STEP
    far = MARGIN + planes

    est_copy = pltpu.make_async_copy(est_hbm, est, local_sem.at[0])
    img_copy = pltpu.make_async_copy(img_hbm, img, local_sem.at[1])
    est_copy.start()
    img_copy.start()

    barrier = pltpu.get_barrier_semaphore()
    count = 0
    for there, who in ((has_down, down), (has_up, up), (has_left, left), (has_right, right)):
        @pl.when(there)
        def _(who=who):
            pl.semaphore_signal(barrier, inc=1, device_id=who, device_id_type=MESH)
        count = count + there.astype(jnp.int32)
    pl.semaphore_wait(barrier, count)

    def est_to(side):
        first = 0 if side == 1 else (planes - MARGIN) * wx
        return pltpu.make_async_remote_copy(
            est_hbm.at[pl.ds(first, MARGIN * wx)], eland.at[side], est_send.at[side], est_recv.at[side],
            device_id=up if side == 0 else down, device_id_type=MESH)

    def smooth_to(it, side):
        src, dst = ((far - MARGIN, 0), (MARGIN, far))[side]
        return pltpu.make_async_remote_copy(
            smooth.at[it, :, :, pl.ds(src, MARGIN)], smooth.at[it, :, :, pl.ds(dst, MARGIN)],
            halo_send.at[it, side], halo_recv.at[it, side],
            device_id=up if side == 0 else down, device_id_type=MESH)

    def edge_to(side, h, k):
        src, dst = ((far - MARGIN, 0), (MARGIN, far))[side]
        xs = pl.ds(k * rows, rows)
        return pltpu.make_async_remote_copy(
            cur.at[1, xs, pl.ds(aligned(src + h * STEP), STEP)], cur.at[1, xs, pl.ds(aligned(dst + h * STEP), STEP)],
            edge_send.at[side, h * n + k], edge_recv.at[side, h * n + k],
            device_id=up if side == 0 else down, device_id_type=MESH)

    sends = ((has_up, has_down), (has_down, has_up))

    for side in range(2):
        @pl.when(sends[side][0])
        def _(side=side):
            est_to(side).start()

    def taps_at(distance, v, a, spacing=1):
        side = halves[v, a, 1]
        for j in range(2, taps):
            side = side + halves[v, a, j]
        total = jnp.full(distance.shape, halves[v, a, 0] + 2.0 * side)
        matrix = jnp.zeros(distance.shape, F32)
        for j in range(taps):
            matrix = jnp.where(distance == j * spacing, halves[v, a, j], matrix)
        return matrix / total

    block = 32

    def build(b, carry):
        start = pl.multiple_of(b * block, block)
        spots_in = pl.ds(start, block)
        r = lax.broadcasted_iota(jnp.int32, (block, wy), 0) + start
        c = lax.broadcasted_iota(jnp.int32, (block, wy), 1)
        for v in range(views):
            hi, lo = halved(taps_at(jnp.abs(r - c), v, 2))
            for part, value in enumerate((hi, hi, lo)):
                ty[v, pl.ds(pl.multiple_of(part * wy + start, block), block), :] = value
        r = lax.broadcasted_iota(jnp.int32, (block, tile), 0) + start
        c = lax.broadcasted_iota(jnp.int32, (block, tile), 1)
        for v in range(views):
            hi, lo = halved(taps_at(jnp.abs(r - c), v, 1, STEP))
            for part, value in enumerate((hi, hi, lo)):
                cx[v, spots_in, pl.ds(part * tile, tile)] = value
        one = jnp.where(c == (r % STEP) * wx + r // STEP, 1.0, 0.0).astype(BF16)
        for part in range(3):
            pm[spots_in, pl.ds(part * tile, tile)] = one
        return carry

    assert wy == tile
    lax.fori_loop(0, wy // block, build, 0)

    window = UNIT + 2 * MARGIN
    p = lax.broadcasted_iota(jnp.int32, (UNIT, 4 * window), 0)
    c = lax.broadcasted_iota(jnp.int32, (UNIT, 4 * window), 1)
    for v in range(views):
        value = taps_at(jnp.abs(c % window - MARGIN - p), v, 0)
        for x in range(2):
            hi, lo = halved(jnp.where((c // window) % 2 == x, value, 0.0))
            dm[pl.ds(v * 4 * UNIT + x * UNIT, UNIT), :] = hi
            dm[pl.ds(v * 4 * UNIT + (2 + x) * UNIT, UNIT), :] = lo

    for side, start in ((0, 0), (1, far)):
        @pl.when(jnp.logical_not(sends[side][1]))
        def _(start=start):
            def clear(x, carry):
                zero = jnp.zeros((MARGIN, wy), F32)
                for it in range(ITERS):
                    cur[it, x, pl.ds(start, MARGIN), :] = zero
                    for v in range(views):
                        smooth[it, v, x, pl.ds(start, MARGIN), :] = zero
                return carry
            lax.fori_loop(0, wx, clear, 0)

    def turned(values):
        return dot(pm[...], jnp.concatenate(thirds(values), 0)).reshape(wx, STEP, wy)

    est_copy.wait()

    def turn_own(b, carry):
        values = est[pl.ds(pl.multiple_of(b * tile, tile), tile), :]
        cur[0, :, pl.ds(pl.multiple_of(MARGIN + b * STEP, STEP), STEP), :] = turned(values)
        return carry

    lax.fori_loop(0, planes // STEP, turn_own, 0, unroll=2)
    img_copy.wait()

    def turn_halo(side):
        @pl.when(sends[side][1])
        def _():
            est_to(side).wait_recv()
            for b in range(MARGIN // STEP):
                start = (0, far)[side] + b * STEP
                cur[0, :, pl.ds(start, STEP), :] = turned(eland[side, pl.ds(b * tile, tile), :])

    def deep_first(it, u):
        def body(j, carry):
            x = 2 * j
            values = cur[it, pl.ds(x, 2), pl.ds(aligned(UNIT * u), window), :].reshape(2 * window, wy)
            got = dot(dm[...], jnp.concatenate(halved(values), 0)).reshape(views, 2, 2, UNIT, wy)
            for v in range(views):
                mid[v, pl.ds(x, 2)] = got[v, 0] + got[v, 1]
            return carry
        lax.fori_loop(0, wx // 2, body, 0, unroll=4)

    def along_y(t, v):
        hi, lo = halved(t)
        return dot(jnp.concatenate([hi, lo, hi], 1), ty[v])

    def along_x(t, v):
        hi, lo = halved(t)
        return dot(cx[v], jnp.concatenate([hi, lo, hi], 0))

    def planar(it, u):
        todo = [(v, h) for h in range(UNIT // STEP) for v in range(views)]
        ts = [mid[v, :, pl.ds(h * STEP, STEP), :].reshape(tile, wy) for v, h in todo]
        ts = [along_y(t, v) for t, (v, h) in zip(ts, todo)]
        ts = [along_x(t, v) for t, (v, h) in zip(ts, todo)]
        pics = [dot(pm[:, :tile], img[v, pl.ds(aligned((u * UNIT + h * STEP) * wx, tile), tile), :]) for v, h in todo]
        ts = [pic / t for t, pic in zip(ts, pics)]
        ts = [along_x(t, v) for t, (v, h) in zip(ts, todo)]
        ts = [along_y(t, v) for t, (v, h) in zip(ts, todo)]
        for t, (v, h) in zip(ts, todo):
            smooth[it, v, :, pl.ds(aligned(MARGIN + u * UNIT + h * STEP), STEP), :] = t.reshape(wx, STEP, wy)

    def forward(it, u):
        deep_first(it, u)
        planar(it, u)

    def deep_last(it, u):
        def body(j, carry):
            x = 2 * j
            got = []
            for v in range(views):
                values = smooth[it, v, pl.ds(x, 2), pl.ds(aligned(UNIT * u), window), :].reshape(2 * window, wy)
                part = dot(dm[pl.ds(v * 4 * UNIT, 4 * UNIT), :], jnp.concatenate(halved(values), 0))
                got.append(part[:2 * UNIT] + part[2 * UNIT:])
            product = got[0]
            for more in got[1:]:
                product = product * more
            fac[pl.ds(x, 2), pl.ds(aligned(UNIT * u), UNIT), :] = product.reshape(2, UNIT, wy)
            return carry
        lax.fori_loop(0, wx // 2, body, 0, unroll=4)

    per_unit = n * (UNIT // STEP)
    items = n * (planes // STEP)

    def place(it, i, goes_left):
        order = ORDERS[it]
        q, h, k = i // per_unit, (i // n) % (UNIT // STEP), i % n
        if it == ITERS - 1 and not goes_left:
            k = n - 1 - k
        u = order[-1]
        for pos in range(len(order) - 1):
            u = jnp.where(q == pos, order[pos], u)
        return u, h, k, pl.ds(k * rows, rows), u * UNIT + h * STEP

    def hop(it, goes_left, xs, ps, i):
        buf_out, buf_in, s, r, who = (
            (to_l, from_r, send_l, recv_r, left) if goes_left else (to_r, from_l, send_r, recv_l, right))
        return pltpu.make_async_remote_copy(
            buf_out.at[xs, ps], buf_in.at[it, xs, ps], s.at[it, i], r.at[it, i], device_id=who, device_id_type=MESH)

    def pass_on(it, i, goes_left):
        _, _, k, xs, first = place(it, i, goes_left)
        ps = pl.ds(aligned(first), STEP)
        live = (i >= 0) & (i < items)
        buf_out, buf_in = (to_l, from_r) if goes_left else (to_r, from_l)
        has_from, has_to = (has_right, has_left) if goes_left else (has_left, has_right)
        if it == ITERS - 1:
            wants = k <= me if goes_left else k >= me
            beyond = k < me if goes_left else k > me
        else:
            wants = beyond = True

        @pl.when(live & has_from & wants)
        def _():
            hop(it, goes_left, xs, ps, i).wait_recv()

        @pl.when(live & has_to & beyond)
        def _():
            @pl.when(has_from)
            def _():
                buf_out[xs, ps, :] = buf_in[it, xs, ps, :] * fac[xs, ps, :]

            @pl.when(jnp.logical_not(has_from))
            def _():
                buf_out[xs, ps, :] = fac[xs, ps, :]

            hop(it, goes_left, xs, ps, i).start()

    def conclude(it, i):
        u, h, k, xs, first = place(it, i, True)
        ps = pl.ds(aligned(first), STEP)
        inner = pl.ds(aligned(MARGIN + first), STEP)
        live = (i >= 0) & (i < items)
        if it == ITERS - 1:
            live = live & (k == me)

        def finish(with_left, with_right):
            total = fac[xs, ps, :] * cur[it, xs, inner, :]
            if with_left:
                total = total * from_l[it, xs, ps, :]
            if with_right:
                total = total * from_r[it, xs, ps, :]
            if it == ITERS - 1:
                out[:, ps, :] = total
            else:
                cur[it + 1, xs, inner, :] = total

        @pl.when(live & jnp.logical_not(has_left))
        def _():
            finish(False, True)

        @pl.when(live & has_left & has_right)
        def _():
            finish(True, True)

        @pl.when(live & jnp.logical_not(has_right))
        def _():
            finish(True, False)

        if it < ITERS - 1:
            @pl.when(live & (u == planes // UNIT - 1) & has_up)
            def _():
                edge_to(0, h, k).start()

            @pl.when(live & (u == 0) & has_down)
            def _():
                edge_to(1, h, k).start()

    def steps(it, begin, end):
        def step(s, carry):
            pass_on(it, s - me, False)
            pass_on(it, s - (n - 1 - me), True)
            if it == ITERS - 1:
                group = s // n
                conclude_now = s % n == n - 1

                @pl.when(conclude_now)
                def _():
                    conclude(it, group * n + me)
            else:
                conclude(it, s - (n - 1))
            return carry
        lax.fori_loop(begin, end, step, 0)

    def settle(it):
        def body(i, carry):
            for goes_left in (False, True):
                _, _, k, xs, first = place(it, i, goes_left)
                ps = pl.ds(aligned(first), STEP)
                has_to = has_left if goes_left else has_right
                beyond = True
                if it == ITERS - 1:
                    beyond = k < me if goes_left else k > me

                @pl.when(has_to & beyond)
                def _():
                    hop(it, goes_left, xs, ps, i).wait_send()
            return carry
        lax.fori_loop(0, items, body, 0)

    def send_smooth(it, side):
        @pl.when(sends[side][0])
        def _():
            smooth_to(it, side).start()

    def get_smooth(it, side):
        @pl.when(sends[side][1])
        def _():
            smooth_to(it, side).wait_recv()

    def get_edge(side):
        @pl.when(sends[side][1])
        def _():
            for h in range(MARGIN // STEP):
                for k in range(n):
                    edge_to(side, h, k).wait_recv()

    forward(0, 1)
    forward(0, 2)
    turn_halo(0)
    forward(0, 0)
    send_smooth(0, 1)
    deep_last(0, 1)
    steps(0, 0, 1)
    turn_halo(1)
    forward(0, 3)
    send_smooth(0, 0)
    steps(0, 1, 2)
    deep_last(0, 2)
    steps(0, 2, 16)
    get_smooth(0, 0)
    deep_last(0, 0)
    steps(0, 16, 24)
    get_smooth(0, 1)
    deep_last(0, 3)
    steps(0, 24, items + n - 1)
    settle(0)

    forward(1, 1)
    forward(1, 2)
    get_edge(1)
    forward(1, 3)
    send_smooth(1, 0)
    deep_last(1, 2)
    steps(1, 0, 1)
    get_edge(0)
    forward(1, 0)
    send_smooth(1, 1)
    steps(1, 1, 2)
    deep_last(1, 1)
    steps(1, 2, 16)
    get_smooth(1, 0)
    deep_last(1, 0)
    steps(1, 16, 24)
    get_smooth(1, 1)
    deep_last(1, 3)
    steps(1, 24, items)
    settle(1)

    for side in range(2):
        @pl.when(sends[side][0])
        def _(side=side):
            est_to(side).wait_send()
            for it in range(ITERS):
                smooth_to(it, side).wait_send()
            for h in range(MARGIN // STEP):
                for k in range(n):
                    edge_to(side, h, k).wait_send()


def solution(mesh):
    n = mesh.shape["view"]

    def on_device(estimate, images, kernel_halves):
        planes, wx, wy = estimate.shape
        views, _, taps = kernel_halves.shape
        rows, tile = wx // n, wx * STEP
        items = n * (planes // STEP)
        deep = planes + 2 * MARGIN
        window = UNIT + 2 * MARGIN
        vmem = pltpu.VMEM
        dma = pltpu.SemaphoreType.DMA
        slab = vmem((wx, planes, wy), F32)
        landing = vmem((ITERS, wx, planes, wy), F32)
        result = pl.pallas_call(
            functools.partial(kernel, (n, planes, wx, wy, views, taps)),
            out_shape=jax.ShapeDtypeStruct((rows, planes, wy), F32),
            in_specs=[pl.BlockSpec(memory_space=pl.ANY), pl.BlockSpec(memory_space=pl.ANY),
                      pl.BlockSpec(memory_space=pltpu.SMEM)],
            out_specs=pl.BlockSpec(memory_space=pltpu.VMEM),
            scratch_shapes=[
                vmem((ITERS, wx, deep, wy), F32),
                vmem((views, wx, UNIT, wy), F32),
                vmem((ITERS, views, wx, deep, wy), F32),
                slab, landing, landing, slab, slab,
                vmem((2, MARGIN * wx, wy), F32),
                vmem((planes * wx, wy), F32),
                vmem((views, planes * wx, wy), BF16),
                vmem((views, 3 * wy, wy), BF16),
                vmem((views, tile, 3 * tile), BF16),
                vmem((views * 4 * UNIT, 4 * window), BF16),
                vmem((tile, 3 * tile), BF16),
                dma((2,)), dma((2,)), dma((2,)),
                dma((ITERS, 2)), dma((ITERS, 2)),
                dma((2, items // 4)), dma((2, items // 4)),
                dma((ITERS, items)), dma((ITERS, items)), dma((ITERS, items)), dma((ITERS, items)),
            ],
            compiler_params=pltpu.CompilerParams(
                collective_id=1, has_side_effects=True, vmem_limit_bytes=56 << 20),
            cost_estimate=pl.CostEstimate(flops=20 << 30, bytes_accessed=5 << 20, transcendentals=0),
        )(estimate.reshape(planes * wx, wy), images.reshape(views, planes * wx, wy), kernel_halves)
        return result.transpose(1, 0, 2)

    placed = (P("space", None, None), P("view", "space", None, None), P("view", None, None))
    return jax.shard_map(
        on_device, mesh=mesh, in_specs=placed, out_specs=P("space", "view", None), check_vma=False
    )
```

profile of v0, /device:TPU:4, one launch (start us, length us, event | category | flops | bytes accessed | tf_op | source)
XLA Modules:
  0.0 222.9 jit_solution(14496761812652196490)
XLA Ops:
  0.0 1.3 copy.4.halves
  1.3 219.4 %shard_map.37 = f32[8,64,256]{2,1,0:T(8,128)} custom-call(f32[2048,256]{1,0:T(8,128)} %bitcast.4, bf16[2,2048,256]{2,1,0:T(8,128)(2,1)} %bitcast.5, f32[2,3,16]{2,1,0:T(4,128)} %copy.4.halves), custom_call_target="tpu_custom_call" | custom-call | flops 21474836480 | bytes 5242880 | tf_op jit(solution)/shard_map/pallas_call | solution.py:427
  220.7 2.1 copy.5
where the time goes:
time: 223 us
  Pallas kernels  219 us (98%)
  local copies, waits for them, and re-layouts  3.42 us (2%)
    pallas_call x1, Pallas kernels, on_device(): pl.pallas_call(functools.partial(kernel, (n, planes, wx, wy, views, taps)...  219 us

commit v1 on v0

--- a/solution.py
+++ b/solution.py
@@ -11,6 +11,7 @@
 MARGIN = 16
 UNIT = 16
 STEP = 8
+LAG = 4
 MESH = pl.DeviceIdType.MESH
 F32, BF16 = jnp.float32, jnp.bfloat16
 ORDERS = ((1, 2, 0, 3), (2, 1, 0, 3))
@@ -234,11 +235,11 @@
             u = jnp.where(q == pos, order[pos], u)
         return u, h, k, pl.ds(k * rows, rows), u * UNIT + h * STEP
 
-    def hop(it, goes_left, xs, ps, i):
+    def hop(it, goes_left, i):
         buf_out, buf_in, s, r, who = (
             (to_l, from_r, send_l, recv_r, left) if goes_left else (to_r, from_l, send_r, recv_l, right))
         return pltpu.make_async_remote_copy(
-            buf_out.at[xs, ps], buf_in.at[it, xs, ps], s.at[it, i], r.at[it, i], device_id=who, device_id_type=MESH)
+            buf_out.at[i], buf_in.at[it, i], s.at[it, i], r.at[it, i], device_id=who, device_id_type=MESH)
 
     def pass_on(it, i, goes_left):
         _, _, k, xs, first = place(it, i, goes_left)
@@ -254,34 +255,35 @@
 
         @pl.when(live & has_from & wants)
         def _():
-            hop(it, goes_left, xs, ps, i).wait_recv()
+            hop(it, goes_left, i).wait_recv()
 
         @pl.when(live & has_to & beyond)
         def _():
             @pl.when(has_from)
             def _():
-                buf_out[xs, ps, :] = buf_in[it, xs, ps, :] * fac[xs, ps, :]
+                buf_out[i] = buf_in[it, i] * fac[xs, ps, :]
 
             @pl.when(jnp.logical_not(has_from))
             def _():
-                buf_out[xs, ps, :] = fac[xs, ps, :]
-
-            hop(it, goes_left, xs, ps, i).start()
+                buf_out[i] = fac[xs, ps, :]
+
+            hop(it, goes_left, i).start()
 
     def conclude(it, i):
         u, h, k, xs, first = place(it, i, True)
         ps = pl.ds(aligned(first), STEP)
         inner = pl.ds(aligned(MARGIN + first), STEP)
         live = (i >= 0) & (i < items)
+        from_left_at = i
         if it == ITERS - 1:
-            live = live & (k == me)
+            from_left_at = i + n - 1 - 2 * k
 
         def finish(with_left, with_right):
             total = fac[xs, ps, :] * cur[it, xs, inner, :]
             if with_left:
-                total = total * from_l[it, xs, ps, :]
+                total = total * from_l[it, from_left_at]
             if with_right:
-                total = total * from_r[it, xs, ps, :]
+                total = total * from_r[it, i]
             if it == ITERS - 1:
                 out[:, ps, :] = total
             else:
@@ -310,25 +312,22 @@
 
     def steps(it, begin, end):
         def step(s, carry):
-            pass_on(it, s - me, False)
-            pass_on(it, s - (n - 1 - me), True)
+            pass_on(it, s - LAG * me, False)
+            pass_on(it, s - LAG * (n - 1 - me), True)
+            done = s - LAG * (n - 1)
             if it == ITERS - 1:
-                group = s // n
-                conclude_now = s % n == n - 1
-
-                @pl.when(conclude_now)
+                @pl.when((done >= 0) & (done % n == 0))
                 def _():
-                    conclude(it, group * n + me)
+                    conclude(it, done + me)
             else:
-                conclude(it, s - (n - 1))
+                conclude(it, done)
             return carry
         lax.fori_loop(begin, end, step, 0)
 
     def settle(it):
         def body(i, carry):
             for goes_left in (False, True):
-                _, _, k, xs, first = place(it, i, goes_left)
-                ps = pl.ds(aligned(first), STEP)
+                _, _, k, _, _ = place(it, i, goes_left)
                 has_to = has_left if goes_left else has_right
                 beyond = True
                 if it == ITERS - 1:
@@ -336,7 +335,7 @@
 
                 @pl.when(has_to & beyond)
                 def _():
-                    hop(it, goes_left, xs, ps, i).wait_send()
+                    hop(it, goes_left, i).wait_send()
             return carry
         lax.fori_loop(0, items, body, 0)
 
@@ -375,7 +374,7 @@
     steps(0, 16, 24)
     get_smooth(0, 1)
     deep_last(0, 3)
-    steps(0, 24, items + n - 1)
+    steps(0, 24, items + LAG * (n - 1))
     settle(0)
 
     forward(1, 1)
@@ -396,7 +395,7 @@
     steps(1, 16, 24)
     get_smooth(1, 1)
     deep_last(1, 3)
-    steps(1, 24, items)
+    steps(1, 24, items + LAG * (n - 1))
     settle(1)
 
     for side in range(2):
@@ -423,7 +422,8 @@
         vmem = pltpu.VMEM
         dma = pltpu.SemaphoreType.DMA
         slab = vmem((wx, planes, wy), F32)
-        landing = vmem((ITERS, wx, planes, wy), F32)
+        outgoing = vmem((items, rows, STEP, wy), F32)
+        landing = vmem((ITERS, items, rows, STEP, wy), F32)
         result = pl.pallas_call(
             functools.partial(kernel, (n, planes, wx, wy, views, taps)),
             out_shape=jax.ShapeDtypeStruct((rows, planes, wy), F32),
@@ -434,7 +434,7 @@
                 vmem((ITERS, wx, deep, wy), F32),
                 vmem((views, wx, UNIT, wy), F32),
                 vmem((ITERS, views, wx, deep, wy), F32),
-                slab, landing, landing, slab, slab,
+                slab, landing, landing, outgoing, outgoing,
                 vmem((2, MARGIN * wx, wy), F32),
                 vmem((planes * wx, wy), F32),
                 vmem((views, planes * wx, wy), BF16),
@@ -444,7 +444,7 @@
                 vmem((tile, 3 * tile), BF16),
                 dma((2,)), dma((2,)), dma((2,)),
                 dma((ITERS, 2)), dma((ITERS, 2)),
-                dma((2, items // 4)), dma((2, items // 4)),
+                dma((2, n * (MARGIN // STEP))), dma((2, n * (MARGIN // STEP))),
                 dma((ITERS, items)), dma((ITERS, items)), dma((ITERS, items)), dma((ITERS, items)),
             ],
             compiler_params=pltpu.CompilerParams(

time: 223 us -> 136 us (0.61); the launches traced: 223 us -> 133 us
  Pallas kernels: 219 us -> 130 us
    pallas_call x1, Pallas kernels: 219 us -> 130 us  [on_device(): pl.pallas_call(functools.partial(kernel, (n, planes, wx, wy, views, taps)...]
where the time goes in v1:
time: 136 us; the launch traced here: 133 us
  Pallas kernels  130 us (96%)
  local copies, waits for them, and re-layouts  3.42 us (3%)
    pallas_call x1, Pallas kernels, on_device(): pl.pallas_call(functools.partial(kernel, (n, planes, wx, wy, views, taps)...  130 us

profile of v1, /device:TPU:4, one launch (start us, length us, event | category | flops | bytes accessed | tf_op | source)
XLA Modules:
  0.0 133.2 jit_solution(7990430591142735615)
XLA Ops:
  0.0 1.3 copy.4.halves
  1.3 129.8 %shard_map.37 = f32[8,64,256]{2,1,0:T(8,128)} custom-call(f32[2048,256]{1,0:T(8,128)} %bitcast.4, bf16[2,2048,256]{2,1,0:T(8,128)(2,1)} %bitcast.5, f32[2,3,16]{2,1,0:T(4,128)} %copy.4.halves), custom_call_target="tpu_custom_call" | custom-call | flops 21474836480 | bytes 5242880 | tf_op jit(solution)/shard_map/pallas_call | solution.py:427
  131.1 2.1 %copy.5 = f32[64,8,256]{2,1,0:T(8,128)} copy(f32[64,8,256]{2,0,1:T(8,128)} %bitcast.3) | data formatting | bytes 1048576 | tf_op jit(solution)/shard_map/transpose | solution.py:454

commit v2 on v1

v2 whole, which is shorter than its diff:
```python
import functools

import jax
import jax.numpy as jnp
from jax import lax
from jax.experimental import pallas as pl
from jax.experimental.pallas import tpu as pltpu
from jax.sharding import PartitionSpec as P

ITERS = 2
MARGIN = 16
UNIT = 16
STEP = 8
LAG = 5
MESH = pl.DeviceIdType.MESH
F32, BF16 = jnp.float32, jnp.bfloat16
NEAR, FAR = 0, 1


def halved(t):
    hi = t.astype(BF16)
    return hi, (t - hi.astype(F32)).astype(BF16)


def thirds(t):
    hi = t.astype(BF16)
    rest = t - hi.astype(F32)
    mid = rest.astype(BF16)
    return hi, mid, (rest - mid.astype(F32)).astype(BF16)


def dot(a, b):
    return jnp.dot(a, b, preferred_element_type=F32)


def aligned(start, multiple=STEP):
    return start if isinstance(start, int) else pl.multiple_of(start, multiple)


def kernel(dims, est_hbm, img_hbm, halves, out, cur, mid, smooth, fac, from_l, from_r, to_r, to_l, eland, est, img,
           ty, cx, dm, dm8, pm, back, local_sem, est_send, est_recv, halo_send, halo_recv, edge_send, edge_recv,
           send_r, recv_l, send_l, recv_r):
    n, planes, wx, wy, views, taps = dims
    me = lax.axis_index("view")
    spot, spots = lax.axis_index("space"), lax.axis_size("space")
    odd = spot % 2 == 1
    toward = jnp.where(odd, -1, 1)
    there = (spot + toward < spots, (spot - toward >= 0) & (spot - toward < spots))
    who = ({"space": jnp.minimum(spot + toward, spots - 1)}, {"space": jnp.clip(spot - toward, 0, spots - 1)})
    has_left, has_right = me > 0, me < n - 1
    right = {"view": jnp.minimum(me + 1, n - 1)}
    left = {"view": jnp.maximum(me - 1, 0)}
    rows = wx // n
    tile = wx * STEP
    deep = planes + 2 * MARGIN

    def unit(f):
        return jnp.where(odd, f, planes // UNIT - 1 - f)

    margin_at = (jnp.where(odd, 0, deep - MARGIN), jnp.where(odd, deep - MARGIN, 0))
    border_at = (jnp.where(odd, MARGIN, deep - 2 * MARGIN), jnp.where(odd, deep - 2 * MARGIN, MARGIN))
    lands_at = (margin_at[FAR], margin_at[NEAR])

    est_copy = pltpu.make_async_copy(est_hbm, est, local_sem.at[0])
    img_copy = pltpu.make_async_copy(img_hbm, img, local_sem.at[1])
    est_copy.start()
    img_copy.start()

    barrier = pltpu.get_barrier_semaphore()
    count = 0
    for here, device in ((there[NEAR], who[NEAR]), (there[FAR], who[FAR]), (has_left, left), (has_right, right)):
        @pl.when(here)
        def _(device=device):
            pl.semaphore_signal(barrier, inc=1, device_id=device, device_id_type=MESH)
        count = count + here.astype(jnp.int32)

    def est_to(side):
        first = (border_at[side] - MARGIN) * wx
        return pltpu.make_async_remote_copy(
            est_hbm.at[pl.ds(aligned(first, MARGIN * wx), MARGIN * wx)], eland.at[side],
            est_send.at[side], est_recv.at[side], device_id=who[side], device_id_type=MESH)

    def piece_at(side, piece):
        return jnp.where(odd == ((side == FAR) == (piece == 0)), STEP, 0)

    def smooth_to(it, side, piece):
        off = piece_at(side, piece)
        return pltpu.make_async_remote_copy(
            smooth.at[it, :, :, pl.ds(aligned(border_at[side] + off), STEP)],
            smooth.at[it, :, :, pl.ds(aligned(lands_at[side] + off), STEP)],
            halo_send.at[it, side, piece], halo_recv.at[it, side, piece], device_id=who[side], device_id_type=MESH)

    def smooth_from(it, side, piece):
        into = smooth.at[it, :, :, pl.ds(aligned(margin_at[side] + STEP - piece_at(side, piece)), STEP)]
        return pltpu.make_async_remote_copy(
            into, into, halo_send.at[it, side, piece], halo_recv.at[it, side, piece],
            device_id=who[side], device_id_type=MESH)

    def edge_to(side, h, k, to=lands_at):
        xs = pl.ds(k * rows, rows)
        return pltpu.make_async_remote_copy(
            cur.at[1, xs, pl.ds(aligned(border_at[side] + h * STEP), STEP)],
            cur.at[1, xs, pl.ds(aligned(to[side] + h * STEP), STEP)],
            edge_send.at[side, h * n + k], edge_recv.at[side, h * n + k],
            device_id=who[side], device_id_type=MESH)

    def taps_at(distance, v, a, spacing=1):
        side = halves[a, v, 1]
        for j in range(2, taps):
            side = side + halves[a, v, j]
        total = jnp.full(distance.shape, halves[a, v, 0] + 2.0 * side)
        matrix = jnp.zeros(distance.shape, F32)
        for j in range(taps):
            matrix = jnp.where(distance == j * spacing, halves[a, v, j], matrix)
        return matrix / total

    block = 32

    def build(b, carry):
        start = pl.multiple_of(b * block, block)
        spots_in = pl.ds(start, block)
        r = lax.broadcasted_iota(jnp.int32, (block, wy), 0) + start
        c = lax.broadcasted_iota(jnp.int32, (block, wy), 1)
        for v in range(views):
            hi, lo = halved(taps_at(jnp.abs(r - c), v, 2))
            for part, value in enumerate((hi, hi, lo)):
                ty[v, pl.ds(pl.multiple_of(part * wy + start, block), block), :] = value
        r = lax.broadcasted_iota(jnp.int32, (block, tile), 0) + start
        c = lax.broadcasted_iota(jnp.int32, (block, tile), 1)
        for v in range(views):
            hi, lo = halved(taps_at(jnp.abs(r - c), v, 1, STEP))
            for part, value in enumerate((hi, hi, lo)):
                cx[v, spots_in, pl.ds(part * tile, tile)] = value
        one = jnp.where(c == (r % STEP) * wx + r // STEP, 1.0, 0.0).astype(BF16)
        for part in range(3):
            pm[spots_in, pl.ds(part * tile, tile)] = one
        return carry

    assert wy == tile
    lax.fori_loop(0, wy // block, build, 0)

    for size, into in ((UNIT, dm), (STEP, dm8)):
        width = size + 2 * MARGIN
        p = lax.broadcasted_iota(jnp.int32, (size, 4 * width), 0)
        c = lax.broadcasted_iota(jnp.int32, (size, 4 * width), 1)
        for v in range(views):
            value = taps_at(jnp.abs(c % width - MARGIN - p), v, 0)
            parts = [halved(jnp.where((c // width) % 2 == x, value, 0.0)) for x in range(2)]
            into[pl.ds(v * 4 * size, 4 * size), :] = jnp.concatenate(
                [parts[0][0], parts[1][0], parts[0][1], parts[1][1]], 0)
    window = UNIT + 2 * MARGIN
    square = rows * STEP
    r = lax.broadcasted_iota(jnp.int32, (square, 3 * square), 0)
    c = lax.broadcasted_iota(jnp.int32, (square, 3 * square), 1) % square
    back[...] = jnp.where(c == (r % rows) * STEP + r // rows, 1.0, 0.0).astype(BF16)

    pl.semaphore_wait(barrier, count)
    for side in (FAR, NEAR):
        @pl.when(there[side])
        def _(side=side):
            est_to(side).start()

    for side in (NEAR, FAR):
        @pl.when(jnp.logical_not(there[side]))
        def _(start=aligned(margin_at[side], MARGIN)):
            def clear(x, carry):
                zero = jnp.zeros((MARGIN, wy), F32)
                for it in range(ITERS):
                    cur[it, x, pl.ds(start, MARGIN), :] = zero
                    for v in range(views):
                        smooth[it, v, x, pl.ds(start, MARGIN), :] = zero
                return carry
            lax.fori_loop(0, wx, clear, 0)

    def turned(values):
        return dot(pm[...], jnp.concatenate(thirds(values), 0)).reshape(wx, STEP, wy)

    est_copy.wait()

    def turn_own(g, carry):
        b = jnp.where(odd, g, planes // STEP - 1 - g)
        values = est[pl.ds(pl.multiple_of(b * tile, tile), tile), :]
        cur[0, :, pl.ds(pl.multiple_of(MARGIN + b * STEP, STEP), STEP), :] = turned(values)
        return carry

    def turn_halo(side):
        @pl.when(there[side])
        def _():
            est_to(side).wait_recv()
            for b in range(MARGIN // STEP):
                start = aligned(margin_at[side] + b * STEP)
                cur[0, :, pl.ds(start, STEP), :] = turned(eland[side, pl.ds(b * tile, tile), :])

    def deep_first(it, u):
        def body(j, carry):
            x = 2 * j
            values = cur[it, pl.ds(x, 2), pl.ds(aligned(UNIT * u), window), :].reshape(2 * window, wy)
            got = dot(dm[...], jnp.concatenate(halved(values), 0)).reshape(views, 2, 2, UNIT, wy)
            for v in range(views):
                mid[v, pl.ds(x, 2)] = got[v, 0] + got[v, 1]
            return carry
        lax.fori_loop(0, wx // 2, body, 0, unroll=4)

    def along_y(t, v):
        hi, lo = halved(t)
        return dot(jnp.concatenate([hi, lo, hi], 1), ty[v])

    def along_x(t, v):
        hi, lo = halved(t)
        return dot(cx[v], jnp.concatenate([hi, lo, hi], 0))

    def planar(it, u):
        todo = [(v, h) for h in range(UNIT // STEP) for v in range(views)]
        ts = [mid[v, :, pl.ds(h * STEP, STEP), :].reshape(tile, wy) for v, h in todo]
        ts = [along_y(t, v) for t, (v, h) in zip(ts, todo)]
        ts = [along_x(t, v) for t, (v, h) in zip(ts, todo)]
        pics = [dot(pm[:, :tile], img[v, pl.ds(aligned((u * UNIT + h * STEP) * wx, tile), tile), :]) for v, h in todo]
        ts = [pic / t for t, pic in zip(ts, pics)]
        ts = [along_x(t, v) for t, (v, h) in zip(ts, todo)]
        ts = [along_y(t, v) for t, (v, h) in zip(ts, todo)]
        for t, (v, h) in zip(ts, todo):
            smooth[it, v, :, pl.ds(aligned(MARGIN + u * UNIT + h * STEP), STEP), :] = t.reshape(wx, STEP, wy)

    def forward(it, u):
        deep_first(it, u)
        planar(it, u)

    def deep_last(it, f, part=None):
        size, matrix = (UNIT, dm) if part is None else (STEP, dm8)
        start = unit(f) * UNIT
        if part is not None:
            start = start + jnp.where(odd == (part == 1), STEP, 0)
        width = size + 2 * MARGIN

        def body(j, carry):
            x = 2 * j
            got = []
            for v in range(views):
                values = smooth[it, v, pl.ds(x, 2), pl.ds(aligned(start), width), :].reshape(2 * width, wy)
                both = dot(matrix[pl.ds(v * 4 * size, 4 * size), :], jnp.concatenate(halved(values), 0))
                got.append(both[:2 * size] + both[2 * size:])
            product = got[0]
            for more in got[1:]:
                product = product * more
            fac[pl.ds(x, 2), pl.ds(aligned(start), size), :] = product.reshape(2, size, wy)
            return carry
        lax.fori_loop(0, wx // 2, body, 0, unroll=4)

    per_unit = n * (UNIT // STEP)
    items = n * (planes // STEP)

    def place(it, i, goes_left):
        f, h, k = i // per_unit, (i // n) % (UNIT // STEP), i % n
        if it == ITERS - 1 and not goes_left:
            k = n - 1 - k
        h = jnp.where(odd, h, UNIT // STEP - 1 - h)
        return f, h, k, pl.ds(k * rows, rows), unit(f) * UNIT + h * STEP

    def hop(it, goes_left, i):
        buf_out, buf_in, s, r, who = (
            (to_l, from_r, send_l, recv_r, left) if goes_left else (to_r, from_l, send_r, recv_l, right))
        return pltpu.make_async_remote_copy(
            buf_out.at[it, i], buf_in.at[it, i], s.at[it], r.at[it, i], device_id=who, device_id_type=MESH)

    def pass_on(it, i, goes_left):
        _, _, k, xs, first = place(it, i, goes_left)
        ps = pl.ds(aligned(first), STEP)
        live = (i >= 0) & (i < items)
        buf_out, buf_in = (to_l, from_r) if goes_left else (to_r, from_l)
        has_from, has_to = (has_right, has_left) if goes_left else (has_left, has_right)
        if it == ITERS - 1:
            wants = k <= me if goes_left else k >= me
            beyond = k < me if goes_left else k > me
        else:
            wants = beyond = True

        @pl.when(live & has_from & wants)
        def _():
            hop(it, goes_left, i).wait_recv()

        @pl.when(live & has_to & beyond)
        def _():
            @pl.when(has_from)
            def _():
                buf_out[it, i] = buf_in[it, i] * fac[xs, ps, :]

            @pl.when(jnp.logical_not(has_from))
            def _():
                buf_out[it, i] = fac[xs, ps, :]

            hop(it, goes_left, i).start()

    def conclude(it, i):
        f, h, k, xs, first = place(it, i, True)
        ps = pl.ds(aligned(first), STEP)
        inner = pl.ds(aligned(MARGIN + first), STEP)
        live = (i >= 0) & (i < items)
        from_left_at = i
        if it == ITERS - 1:
            from_left_at = i + n - 1 - 2 * k

        def finish(with_left, with_right):
            total = fac[xs, ps, :] * cur[it, xs, inner, :]
            if with_left:
                total = total * from_l[it, from_left_at]
            if with_right:
                total = total * from_r[it, i]
            if it == ITERS - 1:
                turned_back = dot(back[...], jnp.concatenate(thirds(total.reshape(rows * STEP, wy)), 0))
                out[pl.ds(aligned(first * rows), rows * STEP), :] = turned_back
            else:
                cur[it + 1, xs, inner, :] = total

        @pl.when(live & jnp.logical_not(has_left))
        def _():
            finish(False, True)

        @pl.when(live & has_left & has_right)
        def _():
            finish(True, True)

        @pl.when(live & jnp.logical_not(has_right))
        def _():
            finish(True, False)

        if it < ITERS - 1:
            for side, border in ((NEAR, 0), (FAR, planes // UNIT - 1)):
                @pl.when(live & (f == border) & there[side])
                def _(side=side):
                    edge_to(side, h, k).start()

    def advance(it, s):
        pass_on(it, s - LAG * me, False)
        pass_on(it, s - LAG * (n - 1 - me), True)
        done = s - LAG * (n - 1)
        if it == ITERS - 1:
            @pl.when((done >= 0) & (done % n == 0))
            def _():
                conclude(it, done + me)
        else:
            conclude(it, done)

    def steps(begin, end, *runs):
        def step(s, carry):
            for it, first in runs:
                advance(it, s + first)
            return carry
        lax.fori_loop(begin, end, step, 0)

    def settle(it):
        for goes_left, buf, sem in ((False, to_r, send_r), (True, to_l, send_l)):
            for place_in in range(n):
                hops = place_in if goes_left else n - 1 - place_in
                if hops == 0:
                    continue
                sent = items if it < ITERS - 1 else hops * (items // n)

                @pl.when(me == place_in)
                def _(goes_left=goes_left, buf=buf, sem=sem, sent=sent):
                    whole = buf.at[it, pl.ds(0, sent)]
                    pltpu.make_async_copy(whole, whole, sem.at[it]).wait()

    def send_smooth(it, side):
        @pl.when(there[side])
        def _():
            for piece in range(2):
                smooth_to(it, side, piece).start()

    def get_smooth(it, side, piece):
        @pl.when(there[side])
        def _():
            smooth_from(it, side, piece).wait_recv()

    def get_edge(side):
        @pl.when(there[side])
        def _():
            for h in range(MARGIN // STEP):
                for k in range(n):
                    edge_to(side, h, k, margin_at).wait_recv()

    drain = LAG * (n - 1)
    last = planes // STEP - 2
    lax.fori_loop(0, last, turn_own, 0, unroll=2)
    img_copy.wait()
    forward(0, unit(1))
    turn_halo(NEAR)
    forward(0, unit(0))
    send_smooth(0, NEAR)
    lax.fori_loop(last, planes // STEP, turn_own, 0, unroll=2)
    deep_first(0, unit(2))
    get_smooth(0, NEAR, 0)
    get_smooth(0, NEAR, 1)
    deep_last(0, 0)
    steps(0, LAG, (0, 0))
    planar(0, unit(2))
    deep_last(0, 1)
    steps(LAG, LAG + 2, (0, 0))
    turn_halo(FAR)
    forward(0, unit(3))
    send_smooth(0, FAR)
    steps(LAG + 2, LAG + 5, (0, 0))
    deep_last(0, 2)
    half = per_unit // 2
    steps(LAG + 5, 3 * per_unit, (0, 0))
    get_smooth(0, FAR, 0)
    deep_last(0, 3, 0)
    steps(3 * per_unit, 3 * per_unit + half, (0, 0))
    get_smooth(0, FAR, 1)
    deep_last(0, 3, 1)
    steps(3 * per_unit + half, 2 * per_unit + drain, (0, 0))

    get_edge(NEAR)
    forward(1, unit(0))
    send_smooth(1, NEAR)
    steps(2 * per_unit + drain, 3 * per_unit + drain, (0, 0))
    forward(1, unit(1))
    get_smooth(1, NEAR, 0)
    get_smooth(1, NEAR, 1)
    deep_last(1, 0)
    steps(0, per_unit, (0, 3 * per_unit + drain), (1, 0))
    forward(1, unit(2))
    deep_last(1, 1)
    steps(per_unit, per_unit + 2, (1, 0))
    get_edge(FAR)
    forward(1, unit(3))
    send_smooth(1, FAR)
    steps(per_unit + 2, per_unit + 4, (1, 0))
    deep_last(1, 2)
    steps(per_unit + 4, 3 * per_unit, (1, 0))
    get_smooth(1, FAR, 0)
    deep_last(1, 3, 0)
    steps(3 * per_unit, 3 * per_unit + half, (1, 0))
    get_smooth(1, FAR, 1)
    deep_last(1, 3, 1)
    steps(3 * per_unit + half, items + drain, (1, 0))
    settle(0)
    settle(1)

    for side in (NEAR, FAR):
        @pl.when(there[side])
        def _(side=side):
            est_to(side).wait_send()
            for it in range(ITERS):
                for piece in range(2):
                    smooth_to(it, side, piece).wait_send()
            for h in range(MARGIN // STEP):
                for k in range(n):
                    edge_to(side, h, k).wait_send()


def solution(mesh):
    n = mesh.shape["view"]

    def on_device(estimate, images, kernel_halves):
        planes, wx, wy = estimate.shape
        views, _, taps = kernel_halves.shape
        rows, tile = wx // n, wx * STEP
        items = n * (planes // STEP)
        deep = planes + 2 * MARGIN
        vmem = pltpu.VMEM
        dma = pltpu.SemaphoreType.DMA
        slab = vmem((wx, planes, wy), F32)
        landing = vmem((ITERS, items, rows, STEP, wy), F32)
        result = pl.pallas_call(
            functools.partial(kernel, (n, planes, wx, wy, views, taps)),
            out_shape=jax.ShapeDtypeStruct((planes * rows, wy), F32),
            in_specs=[pl.BlockSpec(memory_space=pl.ANY), pl.BlockSpec(memory_space=pl.ANY),
                      pl.BlockSpec(memory_space=pltpu.SMEM)],
            out_specs=pl.BlockSpec(memory_space=pltpu.VMEM),
            scratch_shapes=[
                vmem((ITERS, wx, deep, wy), F32),
                vmem((views, wx, UNIT, wy), F32),
                vmem((ITERS, views, wx, deep, wy), F32),
                slab, landing, landing, landing, landing,
                vmem((2, MARGIN * wx, wy), F32),
                vmem((planes * wx, wy), F32),
                vmem((views, planes * wx, wy), BF16),
                vmem((views, 3 * wy, wy), BF16),
                vmem((views, tile, 3 * tile), BF16),
                vmem((views * 4 * UNIT, 4 * (UNIT + 2 * MARGIN)), BF16),
                vmem((views * 4 * STEP, 4 * (STEP + 2 * MARGIN)), BF16),
                vmem((tile, 3 * tile), BF16),
                vmem((rows * STEP, 3 * rows * STEP), BF16),
                dma((2,)), dma((2,)), dma((2,)),
                dma((ITERS, 2, 2)), dma((ITERS, 2, 2)),
                dma((2, n * (MARGIN // STEP))), dma((2, n * (MARGIN // STEP))),
                dma((ITERS,)), dma((ITERS, items)), dma((ITERS,)), dma((ITERS, items)),
            ],
            compiler_params=pltpu.CompilerParams(
                collective_id=1, has_side_effects=True, vmem_limit_bytes=56 << 20),
            cost_estimate=pl.CostEstimate(flops=20 << 30, bytes_accessed=5 << 20, transcendentals=0),
        )(estimate.reshape(planes * wx, wy), images.reshape(views, planes * wx, wy), kernel_halves.transpose(1, 0, 2))
        return result.reshape(planes, rows, wy)

    placed = (P("space", None, None), P("view", "space", None, None), P("view", None, None))
    return jax.shard_map(
        on_device, mesh=mesh, in_specs=placed, out_specs=P("space", "view", None), check_vma=False
    )
```

time: 136 us -> 122 us (0.90); the launches traced: 133 us -> 122 us
  Pallas kernels: 130 us -> 120 us
  local copies, waits for them, and re-layouts: 3.42 us -> 1.87 us
    pallas_call x1, Pallas kernels: 130 us -> 120 us  [on_device(): pl.pallas_call(functools.partial(kernel, (n, planes, wx, wy, views, taps)...]
    transpose x1 -> x0, local copies, waits for them, and re-layouts: 2.14 us -> none  [on_device(): return result.transpose(1, 0, 2)]
where the time goes in v2:
time: 122 us
  Pallas kernels  120 us (98%)
  local copies, waits for them, and re-layouts  1.87 us (2%)
    pallas_call x1, Pallas kernels, on_device(): pl.pallas_call(functools.partial(kernel, (n, planes, wx, wy, views, taps)...  120 us

profile of v2, /device:TPU:4, one launch (start us, length us, event | category | flops | bytes accessed | tf_op | source)
XLA Modules:
  0.0 121.8 jit_solution(13801643306338144198)
XLA Ops:
  0.0 119.9 %shard_map.37 = f32[512,256]{1,0:T(8,128)} custom-call(f32[2048,256]{1,0:T(8,128)} %bitcast.5, bf16[2,2048,256]{2,1,0:T(8,128)(2,1)} %bitcast.6, f32[3,2,16]{2,1,0:T(2,128)} %bitcast.7), custom_call_target="tpu_custom_call" | custom-call | flops 21474836480 | bytes 5242880 | tf_op jit(solution)/shard_map/pallas_call | solution.py:464
  119.9 1.9 %copy.5 = f32[64,8,256]{2,1,0:T(8,128)} copy(f32[64,8,256]{2,1,0:T(8,128)} %bitcast.4) | data formatting | bytes 1048576

commit v3 on v2

--- a/solution.py
+++ b/solution.py
@@ -11,7 +11,7 @@
 MARGIN = 16
 UNIT = 16
 STEP = 8
-LAG = 5
+LAG, SLACK = 3, 0
 MESH = pl.DeviceIdType.MESH
 F32, BF16 = jnp.float32, jnp.bfloat16
 NEAR, FAR = 0, 1
@@ -199,7 +199,7 @@
             for v in range(views):
                 mid[v, pl.ds(x, 2)] = got[v, 0] + got[v, 1]
             return carry
-        lax.fori_loop(0, wx // 2, body, 0, unroll=4)
+        lax.fori_loop(0, wx // 2, body, 0, unroll=16)
 
     def along_y(t, v):
         hi, lo = halved(t)
@@ -244,7 +244,7 @@
                 product = product * more
             fac[pl.ds(x, 2), pl.ds(aligned(start), size), :] = product.reshape(2, size, wy)
             return carry
-        lax.fori_loop(0, wx // 2, body, 0, unroll=4)
+        lax.fori_loop(0, wx // 2, body, 0, unroll=16)
 
     per_unit = n * (UNIT // STEP)
     items = n * (planes // STEP)
@@ -329,10 +329,13 @@
                 def _(side=side):
                     edge_to(side, h, k).start()
 
+    drain = SLACK + LAG * (n - 1)
+    ahead = SLACK + LAG
+
     def advance(it, s):
-        pass_on(it, s - LAG * me, False)
-        pass_on(it, s - LAG * (n - 1 - me), True)
-        done = s - LAG * (n - 1)
+        pass_on(it, s - jnp.where(has_left, SLACK + LAG * me, 0), False)
+        pass_on(it, s - jnp.where(has_right, SLACK + LAG * (n - 1 - me), 0), True)
+        done = s - drain
         if it == ITERS - 1:
             @pl.when((done >= 0) & (done % n == 0))
             def _():
@@ -378,61 +381,93 @@
                 for k in range(n):
                     edge_to(side, h, k, margin_at).wait_recv()
 
-    drain = LAG * (n - 1)
+    taken = [0] * ITERS
+
+    def until(*goals):
+        runs = [[it, taken[it], max(goal, taken[it])] for it, goal in goals]
+        for it, _, goal in runs:
+            taken[it] = goal
+        while any(at < goal for _, at, goal in runs):
+            live = [run for run in runs if run[1] < run[2]]
+            length = min(goal - at for _, at, goal in live)
+            steps(0, length, *[(it, at) for it, at, _ in live])
+            for run in live:
+                run[1] += length
+
+    def more(it, count):
+        until((it, taken[it] + count))
+
+    def factors(it, f):
+        if f == 0:
+            get_smooth(it, NEAR, 0)
+            get_smooth(it, NEAR, 1)
+        deep_last(it, f)
+
+    def far_factors(it, part):
+        get_smooth(it, FAR, part)
+        deep_last(it, 3, part)
+
     last = planes // STEP - 2
-    lax.fori_loop(0, last, turn_own, 0, unroll=2)
+    half = per_unit // 2
+    lax.fori_loop(0, last, turn_own, 0, unroll=3)
     img_copy.wait()
-    forward(0, unit(1))
     turn_halo(NEAR)
     forward(0, unit(0))
     send_smooth(0, NEAR)
+    forward(0, unit(1))
+    factors(0, 0)
+    until((0, ahead))
     lax.fori_loop(last, planes // STEP, turn_own, 0, unroll=2)
     deep_first(0, unit(2))
-    get_smooth(0, NEAR, 0)
-    get_smooth(0, NEAR, 1)
-    deep_last(0, 0)
-    steps(0, LAG, (0, 0))
     planar(0, unit(2))
-    deep_last(0, 1)
-    steps(LAG, LAG + 2, (0, 0))
+    more(0, 1)
+    factors(0, 1)
+    more(0, 1)
     turn_halo(FAR)
-    forward(0, unit(3))
+    deep_first(0, unit(3))
+    more(0, 1)
+    planar(0, unit(3))
     send_smooth(0, FAR)
-    steps(LAG + 2, LAG + 5, (0, 0))
-    deep_last(0, 2)
-    half = per_unit // 2
-    steps(LAG + 5, 3 * per_unit, (0, 0))
-    get_smooth(0, FAR, 0)
-    deep_last(0, 3, 0)
-    steps(3 * per_unit, 3 * per_unit + half, (0, 0))
-    get_smooth(0, FAR, 1)
-    deep_last(0, 3, 1)
-    steps(3 * per_unit + half, 2 * per_unit + drain, (0, 0))
-
+    more(0, 3)
+    factors(0, 2)
+    until((0, 3 * per_unit))
+    far_factors(0, 0)
+    until((0, 3 * per_unit + 2))
+
+    until((0, 2 * per_unit + drain))
     get_edge(NEAR)
-    forward(1, unit(0))
+    deep_first(1, unit(0))
+    until((0, 3 * per_unit + half))
+    far_factors(0, 1)
+    more(0, 1)
+    planar(1, unit(0))
     send_smooth(1, NEAR)
-    steps(2 * per_unit + drain, 3 * per_unit + drain, (0, 0))
-    forward(1, unit(1))
-    get_smooth(1, NEAR, 0)
-    get_smooth(1, NEAR, 1)
-    deep_last(1, 0)
-    steps(0, per_unit, (0, 3 * per_unit + drain), (1, 0))
-    forward(1, unit(2))
-    deep_last(1, 1)
-    steps(per_unit, per_unit + 2, (1, 0))
+    until((0, 3 * per_unit + drain))
+    deep_first(1, unit(1))
+    more(0, 1)
+    planar(1, unit(1))
+    more(0, 1)
+    factors(1, 0)
+    until((1, half), (0, taken[0] + 1))
+    until((1, per_unit - 2), (0, items + drain))
+    deep_first(1, unit(2))
+    more(1, 1)
+    planar(1, unit(2))
+    more(1, 1)
+    factors(1, 1)
+    more(1, 2)
     get_edge(FAR)
-    forward(1, unit(3))
+    deep_first(1, unit(3))
+    more(1, 1)
+    planar(1, unit(3))
     send_smooth(1, FAR)
-    steps(per_unit + 2, per_unit + 4, (1, 0))
-    deep_last(1, 2)
-    steps(per_unit + 4, 3 * per_unit, (1, 0))
-    get_smooth(1, FAR, 0)
-    deep_last(1, 3, 0)
-    steps(3 * per_unit, 3 * per_unit + half, (1, 0))
-    get_smooth(1, FAR, 1)
-    deep_last(1, 3, 1)
-    steps(3 * per_unit + half, items + drain, (1, 0))
+    more(1, 2)
+    factors(1, 2)
+    until((1, 3 * per_unit))
+    far_factors(1, 0)
+    until((1, 3 * per_unit + half))
+    far_factors(1, 1)
+    until((1, items + drain))
     settle(0)
     settle(1)
 

time: 122 us -> 114 us (0.934)
  Pallas kernels: 120 us -> 112 us
    pallas_call x1, Pallas kernels: 120 us -> 112 us  [on_device(): pl.pallas_call(functools.partial(kernel, (n, planes, wx, wy, views, taps)...]
where the time goes in v3:
time: 114 us
  Pallas kernels  112 us (98%)
  local copies, waits for them, and re-layouts  1.87 us (2%)
    pallas_call x1, Pallas kernels, on_device(): pl.pallas_call(functools.partial(kernel, (n, planes, wx, wy, views, taps)...  112 us

profile of v3, /device:TPU:4, one launch (start us, length us, event | category | flops | bytes accessed | tf_op | source)
XLA Modules:
  0.0 114.2 jit_solution(14303683320982970693)
XLA Ops:
  0.0 112.3 %shard_map.37 = f32[512,256]{1,0:T(8,128)} custom-call(f32[2048,256]{1,0:T(8,128)} %bitcast.5, bf16[2,2048,256]{2,1,0:T(8,128)(2,1)} %bitcast.6, f32[3,2,16]{2,1,0:T(2,128)} %bitcast.7), custom_call_target="tpu_custom_call" | custom-call | flops 21474836480 | bytes 5242880 | tf_op jit(solution)/shard_map/pallas_call | solution.py:499
  112.3 1.9 %copy.5 = f32[64,8,256]{2,1,0:T(8,128)} copy(f32[64,8,256]{2,1,0:T(8,128)} %bitcast.4) | data formatting | bytes 1048576

commit v4 on v3

--- a/solution.py
+++ b/solution.py
@@ -416,7 +416,7 @@
     send_smooth(0, NEAR)
     forward(0, unit(1))
     factors(0, 0)
-    until((0, ahead))
+    until((0, ahead + 2))
     lax.fori_loop(last, planes // STEP, turn_own, 0, unroll=2)
     deep_first(0, unit(2))
     planar(0, unit(2))

time: 114 us -> 115 us (level)
  no operation moved by 1% of the time
where the time goes in v4:
time: 115 us
  Pallas kernels  113 us (98%)
  local copies, waits for them, and re-layouts  1.87 us (2%)
    pallas_call x1, Pallas kernels, on_device(): pl.pallas_call(functools.partial(kernel, (n, planes, wx, wy, views, taps)...  113 us

profile of v4, /device:TPU:4, one launch (start us, length us, event | category | flops | bytes accessed | tf_op | source)
XLA Modules:
  0.0 114.8 jit_solution(674945614742407088)
XLA Ops:
  0.0 112.9 %shard_map.37 = f32[512,256]{1,0:T(8,128)} custom-call(f32[2048,256]{1,0:T(8,128)} %bitcast.5, bf16[2,2048,256]{2,1,0:T(8,128)(2,1)} %bitcast.6, f32[3,2,16]{2,1,0:T(2,128)} %bitcast.7), custom_call_target="tpu_custom_call" | custom-call | flops 21474836480 | bytes 5242880 | tf_op jit(solution)/shard_map/pallas_call | solution.py:499
  112.9 1.9 %copy.5 = f32[64,8,256]{2,1,0:T(8,128)} copy(f32[64,8,256]{2,1,0:T(8,128)} %bitcast.4) | data formatting | bytes 1048576
